TPU v7x, 32 devices: a whole 2x2x4 slice. The times are simulated.
32 devices in a mesh: list: 4 (over y, core), shard: 8 (over z, x).
Axes of the slice: x: 2, y: 2, z: 4, core: 2. Of those that a mesh axis runs over, the one named last changes fastest.
Arguments:
- embeddings: bfloat16 [65536, 768], P(('list', 'shard')), may hold values from -6 to 6
- list_ids: int32 [65536, 1], P(('list', 'shard')), may hold values from 0 to 7; in each aligned block of 2048 rows (0 to 2047, 2048 to 4095, ...) at most 256 rows name the same one
- centroids: bfloat16 [8, 1024, 768], P('list'), may hold values from -6 to 6
Outputs:
- new_centroids: float32 [8, 1024, 768], P('list', 'shard')
Inputs may be any that keep to these rules, and one draw needn't show every extreme that they name: `list_ids`: within each device's 2048 rows no coarse list is named by more than 256 rows, a bound that some block reaches.
All inputs are finite; a program needn't handle non-finite values.
Results may differ from a plain program's by a relative error of at most 0.0014.
Values may be sent and summed in bfloat16 or wider, within the bound.
A program may use at most 64 MiB of HBM per device.

v0:
```python
import jax
import jax.numpy as jnp
from jax import lax
from jax.sharding import PartitionSpec as P

SHARP = 0.1
PRIOR = 1.0


def list_stats(block, live, cents):
    raw = jnp.dot(block, cents.T, preferred_element_type=jnp.float32)
    cent_sq = jnp.sum(jnp.square(cents.astype(jnp.float32)), axis=1)
    scores = SHARP * raw - 0.5 * SHARP * cent_sq[None, :]
    resp = jax.nn.softmax(scores, axis=-1) * live[:, None]
    resp = resp.astype(jnp.bfloat16)
    sums = jnp.dot(resp.T, block, preferred_element_type=jnp.float32)
    mass = jnp.sum(resp.astype(jnp.float32), axis=0)
    return (sums, mass)


def per_device(embeddings, list_ids, centroids):
    groups = lax.axis_size("list")
    members = lax.axis_size("shard")
    local_lists = centroids.shape[0]
    fine_count = centroids.shape[1]
    width = centroids.shape[2]
    all_lists = local_lists * groups
    row_count = embeddings.shape[0]
    capacity = row_count // 8
    ids = list_ids[:, 0]
    onehot = (ids[:, None] == jnp.arange(all_lists, dtype=jnp.int32)[None, :]).astype(jnp.int32)
    before = jnp.cumsum(onehot, axis=0) - onehot
    position = jnp.sum(before * onehot, axis=1)
    slot = ids * capacity + position
    outgoing = jnp.zeros((all_lists * capacity, width), jnp.bfloat16).at[slot].set(embeddings)
    occupied = jnp.zeros((all_lists * capacity,), jnp.int32).at[slot].set(1)
    outgoing = outgoing.reshape(groups, local_lists, capacity, width)
    occupied = occupied.reshape(groups, local_lists, capacity)
    arrived, present = (
        lax.all_to_all(outgoing, "list", split_axis=0, concat_axis=0, tiled=True),
        lax.all_to_all(occupied, "list", split_axis=0, concat_axis=0, tiled=True),
    )
    sum_list = []
    mass_list = []
    for index in range(local_lists):
        block = arrived[:, index].reshape(-1, width)
        live_int = present[:, index].reshape(-1)
        sums, mass = list_stats(block, live_int.astype(jnp.float32), centroids[index])
        sum_list.append(sums)
        mass_list.append(mass)
    all_sums = jnp.stack(sum_list, axis=0)
    all_mass = jnp.stack(mass_list, axis=0)
    share_sums, share_mass = (
        lax.psum_scatter(all_sums, "shard", scatter_dimension=1, tiled=True),
        lax.psum_scatter(all_mass, "shard", scatter_dimension=1, tiled=True),
    )
    share = fine_count // members
    start = lax.axis_index("shard") * share
    own = lax.dynamic_slice_in_dim(centroids, start, share, 1).astype(jnp.float32)
    return (share_sums + PRIOR * own) / (share_mass[:, :, None] + PRIOR)


def solution(mesh):
    placed = (P(("list", "shard"), None), P(("list", "shard"), None), P("list", None, None))
    return jax.shard_map(
        per_device, mesh=mesh, in_specs=placed, out_specs=P("list", "shard", None), check_vma=False
    )
```

profile of v0, /device:TPU:12, one launch (start us, length us, event | category | flops | bytes accessed | tf_op | source)
XLA Modules:
  0.0 282.6 jit_solution(8539220390961601175)
XLA Ops:
  6.5 0.7 fusion.15
  7.2 2.3 reduce-window.6
  9.5 0.3 slice_reduce_fusion
  9.8 0.2 reduce-window.9
  10.0 0.1 add_bitcast_fusion
  10.1 0.7 fusion.14
  10.8 0.7 compare_select_fusion
  11.5 8.0 %scatter_custom_fusion.1 = s32[2048]{0:T(1024)S(1)} fusion(s32[2048]{0:T(1024)S(1)} %bitcast.68, s32[2048]{0:T(1024)S(1)} %broadcast.55, s32[]{:T(128)} %constant.15.clone.1), kind=kCustom, calls=%fused_computation.41 | custom fusion | bytes 8196 | tf_op jit(solution)/shard_map/scatter | solution.py:36
  19.6 0.6 reshape.51
  20.2 3.7 %all-to-all-start.1 = ((s32[4,2,256]{2,1,0:T(2,128)}), s32[4,2,256]{2,1,0:T(2,128)S(1)}, u32[]{:S(2)}, u32[]{:S(2)}) async-start(s32[4,2,256]{2,1,0:T(2,128)} %reshape.51), calls=%async_computation.1 | async-start | bytes 16384 | tf_op jit(solution)/shard_map/all_to_all | solution.py:41
  23.9 12.3 %scatter_custom_fusion = bf16[2048,768]{1,0:T(8,128)(2,1)} fusion(s32[2048]{0:T(1024)S(1)} %bitcast.69, bf16[2048,768]{1,0:T(8,128)(2,1)} %param.3, bf16[]{:T(256)} %constant.13.clone.1), kind=kCustom, calls=%fused_computation.23 | custom fusion | bytes 3146240 | tf_op jit(solution)/shard_map/scatter | solution.py:35
  36.2 3.7 %all-to-all-start = ((bf16[4,2,256,768]{3,2,1,0:T(8,128)(2,1)}), bf16[4,2,256,768]{3,2,1,0:T(8,128)(2,1)S(1)}, u32[]{:S(2)}, u32[]{:S(2)}) async-start(bf16[4,2,256,768]{3,2,1,0:T(8,128)(2,1)} %bitcast.5), calls=%async_computation | async-start | bytes 6291456 | tf_op jit(solution)/shard_map/all_to_all | solution.py:40
  39.9 0.2 reduce-scatter.7.cloned.1.call-start
  40.1 2.6 multiply_reduce_fusion.1
  42.7 32.5 %all-to-all-done = bf16[4,2,256,768]{3,2,1,0:T(8,128)(2,1)S(1)} async-done(((bf16[4,2,256,768]{3,2,1,0:T(8,128)(2,1)}), bf16[4,2,256,768]{3,2,1,0:T(8,128)(2,1)S(1)}, u32[]{:S(2)}, u32[]{:S(2)}) %all-to-all-start) | async-done | bytes 3145760 | tf_op jit(solution)/shard_map/all_to_all | solution.py:40
  75.2 0.2 fusion.18
  75.4 2.8 copy-done
  78.2 1.8 fusion
  80.1 0.9 fusion.2
  81.0 1.8 convert_reduce_fusion.1
  82.8 1.8 fusion.1
  84.7 0.9 fusion.3
  85.6 2.8 convert_reduce_fusion
  88.4 1.0 copy.4
  89.5 0.0 reduce-scatter.5.cloned.1.call-start
  89.5 3.3 %convolution_bitcast_fusion.1 = f32[1,1024,768]{2,1,0:T(8,128)S(1)} fusion(bf16[1024,1024]{0,1:T(8,128)(2,1)S(1)} %get-tuple-element.8, bf16[1024,768]{1,0:T(8,128)(2,1)} %bitcast.58), kind=kOutput, calls=%fused_computation.18 | convolution fusion | flops 1610612736 | bytes 6815744 | tf_op jit(solution)/shard_map/dot_general | solution.py:16
  92.9 1.8 convolution_bitcast_fusion
  94.7 3.1 %pad_maximum_fusion = f32[2,1024,768]{2,1,0:T(8,128)} fusion(f32[1,1024,768]{2,1,0:T(8,128)S(1)} %convolution_bitcast_fusion, f32[1,1024,768]{2,1,0:T(8,128)S(1)} %convolution_bitcast_fusion.1), kind=kLoop, calls=%fused_computation.2 | loop fusion | flops 1572864 | bytes 12582912 | tf_op jit(solution)/shard_map/stack | solution.py:51
  97.8 55.4 %reduce-scatter.7.cloned.1.call-done = f32[128,2]{1,0:T(8,128)} async-done(((f32[1024,2]{1,0:T(8,128)}), f32[128,2]{1,0:T(8,128)}) %reduce-scatter.7.cloned.1.call-update) | async-done | bytes 1040
  153.2 0.9 copy.5
  154.1 119.4 %reduce-scatter.5.cloned.1.call-done = f32[2,128,768]{2,1,0:T(8,128)} async-done(((f32[2,1024,768]{2,1,0:T(8,128)}), f32[2,128,768]{2,1,0:T(8,128)}) %reduce-scatter.5.cloned.1.call-update) | async-done | bytes 786448 | tf_op jit(solution)/shard_map/reduce_scatter | solution.py:54
  273.5 2.2 add_divide_fusion
  (17 shorter events, 0.1 us)
Async XLA Ops:
  20.2 16.0 %all-to-all-start.1 = ((s32[4,2,256]{2,1,0:T(2,128)}), s32[4,2,256]{2,1,0:T(2,128)S(1)}, u32[]{:S(2)}, u32[]{:S(2)}) async-start(s32[4,2,256]{2,1,0:T(2,128)} %reshape.51), calls=%async_computation.1 | async-start | bytes 16384 | tf_op jit(solution)/shard_map/all_to_all | solution.py:41
  36.2 39.0 %all-to-all-start = ((bf16[4,2,256,768]{3,2,1,0:T(8,128)(2,1)}), bf16[4,2,256,768]{3,2,1,0:T(8,128)(2,1)S(1)}, u32[]{:S(2)}, u32[]{:S(2)}) async-start(bf16[4,2,256,768]{3,2,1,0:T(8,128)(2,1)} %bitcast.5), calls=%async_computation | async-start | bytes 6291456 | tf_op jit(solution)/shard_map/all_to_all | solution.py:40
  39.9 113.3 %reduce-scatter.7.cloned.1.call-start = ((), (), s32[]{:S(2)}) async-start(), calls=%async_computation.5 | async-start | bytes 589824
  75.2 3.0 %copy-start = (bf16[2,1024,768]{2,1,0:T(8,128)(2,1)S(1)}, bf16[2,1024,768]{2,1,0:T(8,128)(2,1)}, u32[]{:S(2)}) copy-start(bf16[2,1024,768]{2,1,0:T(8,128)(2,1)} %param.5) | copy-start | bytes 9437188
  75.4 4.7 %copy-start.4 = (bf16[4,1,256,768]{3,2,1,0:T(8,128)(2,1)}, bf16[4,1,256,768]{3,2,1,0:T(8,128)(2,1)S(1)}, u32[]{:S(2)}) copy-start(bf16[4,1,256,768]{3,2,1,0:T(8,128)(2,1)S(1)} %get-tuple-element.11) | copy-start | bytes 4718596
  75.4 7.4 %copy-start.2 = (bf16[4,1,256,768]{3,2,1,0:T(8,128)(2,1)}, bf16[4,1,256,768]{3,2,1,0:T(8,128)(2,1)S(1)}, u32[]{:S(2)}) copy-start(bf16[4,1,256,768]{3,2,1,0:T(8,128)(2,1)S(1)} %get-tuple-element.12) | copy-start | bytes 4718596
  89.5 184.0 %reduce-scatter.5.cloned.1.call-start = ((), (), s32[]{:S(2)}) async-start(), calls=%async_computation.4 | async-start | bytes 7077888 | tf_op jit(solution)/shard_map/reduce_scatter | solution.py:54
  89.5 3.4 %copy-start.1 = (bf16[1024,1024]{0,1:T(8,128)(2,1)S(1)}, bf16[1024,1024]{0,1:T(8,128)(2,1)}, u32[]{:S(2)}) copy-start(bf16[1024,1024]{0,1:T(8,128)(2,1)} %get-tuple-element.10) | copy-start | bytes 6291460
  89.5 3.4 %copy-start.3 = (bf16[4,1,256,768]{3,2,1,0:T(8,128)(2,1)S(1)}, bf16[4,1,256,768]{3,2,1,0:T(8,128)(2,1)}, u32[]{:S(2)}) copy-start(bf16[4,1,256,768]{3,2,1,0:T(8,128)(2,1)} %copy-done.2) | copy-start | bytes 4718596
Sparse Core Ops, SparseCore 0:
  89.6 63.5 reduce-scatter.6
  157.2 116.2 reduce-scatter.4
where the time goes:
time: 285 us; the launch traced here: 283 us
  waiting for transfers between devices  207 us (73%)
  local copies, waits for them, and re-layouts  26.2 us (9%)
  other arithmetic  19 us (7%)
  between operations  13.6 us (5%)
  matrix products  8.82 us (3%)
  starting transfers between devices  7.69 us (3%)
    reduce_scatter x1, waiting for transfers between devices, per_device(): lax.psum_scatter(all_sums, 'shard', scatter_dimension=1, tiled=True)  119 us
    unnamed x3, waiting for transfers between devices  55.4 us
    all_to_all x1, waiting for transfers between devices, per_device(): lax.all_to_all(outgoing, 'list', split_axis=0, concat_axis=0, tiled=True)  32.5 us
    scatter x1, local copies, waits for them, and re-layouts, per_device(): jnp.zeros((all_lists * capacity, width), jnp.bfloat16).at[slot]  12.3 us
    scatter x1, local copies, waits for them, and re-layouts, per_device(): occupied = jnp.zeros((all_lists * capacity,), jnp.int32).at[slot].set(1)  8.05 us
  transfers between devices with their start and end apart: 4, of which 3 were waited for; matrix products, arithmetic and copies ran while one was open for 8% of the time, Pallas kernels for 0%

commit v1 on v0

v1 whole, which is shorter than its diff:
```python
import functools

import jax
import jax.numpy as jnp
from jax import lax
from jax.experimental import pallas as pl
from jax.experimental.pallas import tpu as pltpu
from jax.sharding import PartitionSpec as P

SHARP = 0.1
PRIOR = 1.0
MESH = pl.DeviceIdType.MESH
F32 = jnp.float32
BF16 = jnp.bfloat16
CORES = 2


def iota(shape, axis):
    return lax.broadcasted_iota(jnp.int32, shape, axis)


def dot(a, b):
    return jnp.dot(a, b, preferred_element_type=F32)


def kernel(
    n_list, n_shard, full,
    ids_ref, emb_ref, cent_ref, out_ref,
    slot_s, send, recv, cbuf, csq, acc,
    part, mpart, other, mother, merged, mmerged, fin, mfin,
    cent_sem, p1_send, p1_recv, part_send, part_recv, mp_sem,
    fin_send, fin_recv, mf_send, mf_recv,
):
    local_lists, fine, width = cent_ref.shape
    quad = local_lists * CORES
    planes = n_list // CORES
    lists = planes * quad
    groups = n_shard // quad
    halves = n_shard // CORES
    per_group = quad // CORES
    share = fine // n_shard
    rows = emb_ref.shape[0]
    cap = rows // 8
    li, sh = lax.axis_index("list"), lax.axis_index("shard")
    y, core = li // CORES, li % CORES
    group, member = sh // quad, sh % quad
    home, hidx = member // local_lists, member % local_lists
    partner = {"list": y * CORES + (1 - core), "shard": sh}

    barrier = pltpu.get_barrier_semaphore()
    in_plane = CORES * n_shard

    def greet_plane(i, c):
        at = (core * n_shard + sh + i) % in_plane
        pl.semaphore_signal(
            barrier, inc=1, device_id={"list": y * CORES + at // n_shard, "shard": at % n_shard}, device_id_type=MESH
        )
        return c

    def greet_far(i, c):
        to_y = (y + 1 + i // quad) % planes
        pl.semaphore_signal(
            barrier, inc=1, device_id={"list": to_y * CORES + core, "shard": group * quad + i % quad}, device_id_type=MESH
        )
        return c

    lax.fori_loop(1, in_plane, greet_plane, 0)
    lax.fori_loop(0, (planes - 1) * quad, greet_far, 0)

    ids = ids_ref[...]
    blocks, lane = ids.shape
    hot = [jnp.where(ids == l, 1.0, 0.0).astype(F32) for l in range(lists)]
    hots = jnp.concatenate(hot, axis=0).astype(BF16)
    many = lists * blocks
    before = jnp.where(iota((lane, lane), 0) < iota((lane, lane), 1), 1.0, 0.0).astype(BF16)
    rank = dot(hots, before)
    totals = dot(hots, jnp.ones((lane, lane), BF16)).astype(BF16)
    up, down = iota((many, many), 0), iota((many, many), 1)
    earlier = jnp.where((up // blocks == down // blocks) & (down < up), 1.0, 0.0).astype(BF16)
    rank = rank + dot(earlier, totals)
    slot = jnp.zeros((blocks, lane), F32)
    for l in range(lists):
        slot = slot + hot[l] * (rank[l * blocks:(l + 1) * blocks] + float(l * cap))
    slot_s[...] = slot

    pl.semaphore_wait(barrier, in_plane - 1 + (planes - 1) * quad)

    cent_far = pltpu.make_async_remote_copy(
        src_ref=cent_ref.at[hidx], dst_ref=cbuf, send_sem=cent_sem.at[0], recv_sem=cent_sem.at[1],
        device_id=partner, device_id_type=MESH,
    )
    cent_near = pltpu.make_async_copy(cent_ref.at[hidx], cbuf, cent_sem.at[2])

    @pl.when(core == home)
    def _():
        cent_far.start()
        cent_near.start()

    def gather_rows(l, dst):
        base = (l * cap).astype(F32)
        place = iota((cap, lane), 0).astype(F32) + base
        pick = jnp.concatenate(
            [jnp.where(place == slot_s[b:b + 1, :], 1.0, 0.0).astype(BF16) for b in range(blocks)], axis=1
        )
        dst[:, :width] = dot(pick, emb_ref[...]).astype(BF16)
        if not full:
            dst[:, width:] = dot(pick, jnp.ones((rows, 128), BF16)).astype(BF16)

    def order(i):
        return (5 * i) % lists

    def row_copy(j):
        to_y, to_member = (y + j // quad) % planes, (member + j % quad) % quad
        return pltpu.make_async_remote_copy(
            src_ref=send.at[j], dst_ref=recv.at[j], send_sem=p1_send.at[j], recv_sem=p1_recv.at[j],
            device_id={"list": to_y * CORES + core, "shard": group * quad + to_member}, device_id_type=MESH,
        )

    def route(i, c):
        j = order(i)
        to_y, to_member = (y + j // quad) % planes, (member + j % quad) % quad
        gather_rows(to_y * quad + to_member, send.at[j])
        row_copy(j).start()
        return c

    lax.fori_loop(1, lists, route, 0)
    gather_rows(y * quad + member, recv.at[0])

    @pl.when(core == home)
    def _():
        cent_near.wait()

    @pl.when(core != home)
    def _():
        cent_far.wait_recv()

    def square(i, c):
        at = pl.ds(pl.multiple_of(i * 128, 128), 128)
        some = cbuf[at, :].astype(F32)
        csq[at, :] = jnp.broadcast_to((0.5 * SHARP) * jnp.sum(some * some, axis=1, keepdims=True), (128, cap))
        return c

    lax.fori_loop(0, fine // 128, square, 0)
    acc[...] = jnp.zeros_like(acc)

    def add_block(j):
        x = recv[j, :, :width]
        flags = jnp.ones((cap, 128), BF16) if full else recv[j, :, width:]
        raw = lax.dot_general(cbuf[...], x, (((1,), (1,)), ((), ())), preferred_element_type=F32)
        scores = SHARP * raw - csq[...]
        grown = jnp.exp(scores - jnp.max(scores, axis=0, keepdims=True))
        resp = (grown * (1.0 / jnp.sum(grown, axis=0, keepdims=True))).astype(BF16)
        acc[:, :width] += dot(resp, x)
        acc[:, width:] += dot(resp, flags)

    add_block(0)

    def take(i, c):
        j = order(i)
        row_copy(j).wait_recv()
        add_block(j)
        return c

    lax.fori_loop(1, lists, take, 0)

    eye = iota((share, 128), 0) == iota((share, 128), 1)

    def pair(t):
        return ((group + 1 + t // per_group) % groups) * per_group + (t + sh // CORES) % per_group

    def fine_rows(shard):
        return pl.ds(pl.multiple_of(shard * share, share), share)

    def mass_row(at):
        tile = acc[at, width:]
        return jnp.broadcast_to(jnp.sum(jnp.where(eye, tile, 0.0), axis=0, keepdims=True), (8, 128))

    def part_copy(t):
        return pltpu.make_async_remote_copy(
            src_ref=part.at[t], dst_ref=other.at[t], send_sem=part_send.at[t], recv_sem=part_recv.at[t],
            device_id=partner, device_id_type=MESH,
        )

    mass_copy = pltpu.make_async_remote_copy(
        src_ref=mpart, dst_ref=mother, send_sem=mp_sem.at[0], recv_sem=mp_sem.at[1],
        device_id=partner, device_id_type=MESH,
    )

    def give(t, c):
        at = fine_rows(CORES * pair(t) + (1 - core))
        part[t] = acc[at, :width].astype(BF16)
        part_copy(t).start()
        mpart[t] = mass_row(at)
        return c

    lax.fori_loop(0, halves, give, 0)
    mass_copy.start()

    def fin_copies(t):
        to = {"list": y * CORES + home, "shard": CORES * pair(t) + core}
        at = hidx * groups + group
        return [
            pltpu.make_async_remote_copy(
                src_ref=src.at[t], dst_ref=dst.at[at], send_sem=ss.at[t], recv_sem=rs.at[at],
                device_id=to, device_id_type=MESH,
            )
            for src, dst, ss, rs in ((merged, fin, fin_send, fin_recv), (mmerged, mfin, mf_send, mf_recv))
        ]

    def own_copies(t):
        at = hidx * groups + group
        return [
            pltpu.make_async_copy(merged.at[t], fin.at[at], fin_recv.at[at]),
            pltpu.make_async_copy(mmerged.at[t], mfin.at[at], mf_recv.at[at]),
        ]

    def is_own(t):
        return (home == core) & (CORES * pair(t) + core == sh)

    mass_copy.wait_recv()

    def forward(t, c):
        at = fine_rows(CORES * pair(t) + core)
        part_copy(t).wait_recv()
        merged[t] = (acc[at, :width] + other[t].astype(F32)).astype(BF16)
        mmerged[t] = mass_row(at) + mother[t]

        @pl.when(is_own(t))
        def _():
            for copy in own_copies(t):
                copy.start()

        @pl.when(jnp.logical_not(is_own(t)))
        def _():
            for copy in fin_copies(t):
                copy.start()

        return c

    lax.fori_loop(0, halves, forward, 0)

    @pl.when(core == home)
    def _():
        cent_far.wait_send()

    def sent_rows(i, c):
        row_copy(order(i)).wait_send()
        return c

    lax.fori_loop(1, lists, sent_rows, 0)

    def sent_parts(t, c):
        part_copy(t).wait_send()
        return c

    lax.fori_loop(0, halves, sent_parts, 0)
    mass_copy.wait_send()

    def arrived(i):
        return [
            pltpu.make_async_copy(fin.at[i], fin.at[i], fin_recv.at[i]),
            pltpu.make_async_copy(mfin.at[i], mfin.at[i], mf_recv.at[i]),
        ]

    for h in range(local_lists):
        sums = cent_ref[h, fine_rows(sh), :].astype(F32) * PRIOR
        mass = jnp.zeros((1, 128), F32)
        for k in range(groups):
            i = h * groups + k
            for copy in arrived(i):
                copy.wait()
            sums = sums + fin[i].astype(F32)
            mass = mass + mfin[i, 0:1, :]
        column = jnp.sum(jnp.where(eye, mass, 0.0), axis=1, keepdims=True)
        out_ref[h] = sums / (column + PRIOR)

    def sent_fin(t, c):
        @pl.when(jnp.logical_not(is_own(t)))
        def _():
            for copy in fin_copies(t):
                copy.wait_send()

        return c

    lax.fori_loop(0, halves, sent_fin, 0)


def solution(mesh):
    n_list, n_shard = mesh.shape["list"], mesh.shape["shard"]

    def per_device(embeddings, list_ids, centroids):
        rows, width = embeddings.shape
        local_lists, fine, _ = centroids.shape
        cap = rows // 8
        lists = local_lists * n_list
        full = lists * cap == rows
        sent = width if full else width + 128
        share = fine // n_shard
        halves = n_shard // CORES
        arrivals = local_lists * (n_shard // (local_lists * CORES))
        dma = pltpu.SemaphoreType.DMA
        vmem = pl.BlockSpec(memory_space=pltpu.VMEM)
        flops = 2 * rows * lists * cap * width + 4 * lists * cap * fine * width
        return pl.pallas_call(
            functools.partial(kernel, n_list, n_shard, full),
            out_shape=jax.ShapeDtypeStruct((local_lists, share, width), F32),
            in_specs=[vmem, vmem, vmem],
            out_specs=vmem,
            scratch_shapes=[
                pltpu.VMEM((rows // cap, cap), F32),
                pltpu.VMEM((lists, cap, sent), BF16),
                pltpu.VMEM((lists, cap, sent), BF16),
                pltpu.VMEM((fine, width), BF16),
                pltpu.VMEM((fine, cap), F32),
                pltpu.VMEM((fine, width + 128), F32),
                pltpu.VMEM((halves, share, width), BF16),
                pltpu.VMEM((halves, 8, 128), F32),
                pltpu.VMEM((halves, share, width), BF16),
                pltpu.VMEM((halves, 8, 128), F32),
                pltpu.VMEM((halves, share, width), BF16),
                pltpu.VMEM((halves, 8, 128), F32),
                pltpu.VMEM((arrivals, share, width), BF16),
                pltpu.VMEM((arrivals, 8, 128), F32),
                dma((3,)),
                dma((lists,)),
                dma((lists,)),
                dma((halves,)),
                dma((halves,)),
                dma((2,)),
                dma((halves,)),
                dma((arrivals,)),
                dma((halves,)),
                dma((arrivals,)),
            ],
            compiler_params=pltpu.CompilerParams(
                collective_id=0, has_side_effects=True, vmem_limit_bytes=52 * 2**20
            ),
            cost_estimate=pl.CostEstimate(
                flops=flops, bytes_accessed=4 * rows * width, transcendentals=lists * cap * fine
            ),
        )(list_ids.reshape(rows // cap, cap), embeddings, centroids)

    placed = (P(("list", "shard"), None), P(("list", "shard"), None), P("list", None, None))
    return jax.shard_map(
        per_device, mesh=mesh, in_specs=placed, out_specs=P("list", "shard", None), check_vma=False
    )
```

time: 285 us -> 78.7 us (0.28)
  waiting for transfers between devices: 207 us -> 0 us
  Pallas kernels: 0 us -> 74.4 us
  local copies, waits for them, and re-layouts: 26.2 us -> 1.4 us
  other arithmetic: 19 us -> 1.36 us
  between operations: 13.6 us -> 0.02 us
  matrix products: 8.82 us -> 0 us
  starting transfers between devices: 7.69 us -> 0 us
    reduce_scatter x1 -> x0, waiting for transfers between devices: 119 us -> none  [per_device(): lax.psum_scatter(all_sums, 'shard', scatter_dimension=1, tiled=True)]
    pallas_call x0 -> x1, Pallas kernels: none -> 74.4 us  [per_device(): pl.pallas_call(functools.partial(kernel, n_list, n_shard, full), out_shap...]
    unnamed x3 -> x0, waiting for transfers between devices: 55.4 us -> none
    all_to_all x2 -> x0, waiting for transfers between devices: 32.5 us -> none  [the longest x1 32.5 us: per_device(): lax.all_to_all(outgoing, 'list', split_axis=0, concat_axis=0, tiled=True)]
    scatter x2 -> x0, local copies, waits for them, and re-layouts: 20.3 us -> none  [the longest x1 12.3 us: per_device(): jnp.zeros((all_lists * capacity, width), jnp.bfloat16).at[slot]]
    reduce_sum x6 -> x0, other arithmetic: 9.74 us -> none  [the longest x2 4.65 us: list_stats(): mass = jnp.sum(resp.astype(jnp.float32), axis=0)]
    dot_general x4 -> x0, matrix products: 8.82 us -> none  [the longest x2 5.15 us: list_stats(): sums = jnp.dot(resp.T, block, preferred_element_type=jnp.float32)]
    all_to_all x2 -> x0, starting transfers between devices: 7.44 us -> none  [the longest x1 3.72 us: per_device(): lax.all_to_all(occupied, 'list', split_axis=0, concat_axis=0, tiled=True)]
  transfers between devices with their start and end apart: 4 -> 0, of which waited for: 3 -> 0; matrix products, arithmetic and copies ran while one was open for 8% -> 0% of each run, Pallas kernels for 0% -> 0%
where the time goes in v1:
time: 78.7 us; the launch traced here: 77.1 us
  Pallas kernels  74.4 us (95%)
  local copies, waits for them, and re-layouts  1.4 us (2%)
  other arithmetic  1.36 us (2%)
    pallas_call x1, Pallas kernels, per_device(): pl.pallas_call(functools.partial(kernel, n_list, n_shard, full), out_shap...  74.4 us

profile of v1, /device:TPU:12, one launch (start us, length us, event | category | flops | bytes accessed | tf_op | source)
XLA Modules:
  0.0 77.1 jit_solution(15294707793201073763)
XLA Ops:
  0.0 0.5 broadcast.3
  0.5 1.4 %reduce.3 = s32[2048]{0:T(1024)S(1)} reduce(s32[2048,1]{0,1:T(1,128)} %param.4, s32[]{:T(128)} %broadcast.3), dimensions={1}, to_apply=%param.4.reduce_sub_computation.3 | reduce | bytes 16388 | tf_op args[1]
  1.9 74.4 %shard_map.37 = f32[2,128,768]{2,1,0:T(8,128)S(1)} custom-call(s32[8,256]{1,0:T(8,128)S(1)} %reshape.3.ids_ref, bf16[2048,768]{1,0:T(8,128)(2,1)} %emb_ref.1, bf16[2,1024,768]{2,1,0:T(8,128)(2,1)} %cent_ref.1), custom_call_target="tpu_custom_call" | custom-call | flops 12884901888 | bytes 6291456 | tf_op jit(solution)/shard_map/pallas_call | solution.py:304
  76.3 0.9 %copy.5 = f32[2,128,768]{2,1,0:T(8,128)} copy(f32[2,128,768]{2,1,0:T(8,128)S(1)} %shard_map.37) | data formatting | bytes 1572864
  (1 shorter events, 0.0 us)

commit v2 on v1

--- a/solution.py
+++ b/solution.py
@@ -13,6 +13,7 @@
 F32 = jnp.float32
 BF16 = jnp.bfloat16
 CORES = 2
+AHEAD = 3
 
 
 def iota(shape, axis):
@@ -26,9 +27,9 @@
 def kernel(
     n_list, n_shard, full,
     ids_ref, emb_ref, cent_ref, out_ref,
-    slot_s, send, recv, cbuf, csq, acc,
+    emb_s, own_s, slot_s, send, recv, cbuf, csq, acc,
     part, mpart, other, mother, merged, mmerged, fin, mfin,
-    cent_sem, p1_send, p1_recv, part_send, part_recv, mp_sem,
+    in_sem, cent_sem, p1_send, p1_recv, part_send, part_recv, mp_sem,
     fin_send, fin_recv, mf_send, mf_recv,
 ):
     local_lists, fine, width = cent_ref.shape
@@ -47,6 +48,13 @@
     home, hidx = member // local_lists, member % local_lists
     partner = {"list": y * CORES + (1 - core), "shard": sh}
 
+    emb_in = pltpu.make_async_copy(emb_ref, emb_s, in_sem.at[0])
+    own_in = pltpu.make_async_copy(
+        cent_ref.at[:, pl.ds(pl.multiple_of(sh * share, share), share), :], own_s, in_sem.at[1]
+    )
+    emb_in.start()
+    own_in.start()
+
     barrier = pltpu.get_barrier_semaphore()
     in_plane = CORES * n_shard
 
@@ -67,8 +75,8 @@
     lax.fori_loop(1, in_plane, greet_plane, 0)
     lax.fori_loop(0, (planes - 1) * quad, greet_far, 0)
 
-    ids = ids_ref[...]
-    blocks, lane = ids.shape
+    blocks, lane = rows // cap, cap
+    ids = jnp.concatenate([ids_ref[:, b * lane:(b + 1) * lane] for b in range(blocks)], axis=0)
     hot = [jnp.where(ids == l, 1.0, 0.0).astype(F32) for l in range(lists)]
     hots = jnp.concatenate(hot, axis=0).astype(BF16)
     many = lists * blocks
@@ -83,6 +91,7 @@
         slot = slot + hot[l] * (rank[l * blocks:(l + 1) * blocks] + float(l * cap))
     slot_s[...] = slot
 
+    emb_in.wait()
     pl.semaphore_wait(barrier, in_plane - 1 + (planes - 1) * quad)
 
     cent_far = pltpu.make_async_remote_copy(
@@ -102,28 +111,40 @@
         pick = jnp.concatenate(
             [jnp.where(place == slot_s[b:b + 1, :], 1.0, 0.0).astype(BF16) for b in range(blocks)], axis=1
         )
-        dst[:, :width] = dot(pick, emb_ref[...]).astype(BF16)
+        dst[:, :width] = dot(pick, emb_s[...]).astype(BF16)
         if not full:
             dst[:, width:] = dot(pick, jnp.ones((rows, 128), BF16)).astype(BF16)
 
     def order(i):
-        return (5 * i) % lists
+        return lists // 2 + i // 2 - (i % 2) * (2 * (i // 2) + 1)
+
+    def target(j):
+        flip = j % quad
+        to_member = ((member // 2 + flip // 2) % (quad // 2)) * 2 + (member + flip) % 2
+        return (y + j // quad) % planes, to_member
 
     def row_copy(j):
-        to_y, to_member = (y + j // quad) % planes, (member + j % quad) % quad
+        to_y, to_member = target(j)
         return pltpu.make_async_remote_copy(
             src_ref=send.at[j], dst_ref=recv.at[j], send_sem=p1_send.at[j], recv_sem=p1_recv.at[j],
             device_id={"list": to_y * CORES + core, "shard": group * quad + to_member}, device_id_type=MESH,
         )
 
+    def prepare(i):
+        to_y, to_member = target(order(i))
+        gather_rows(to_y * quad + to_member, send.at[order(i)])
+
     def route(i, c):
-        j = order(i)
-        to_y, to_member = (y + j // quad) % planes, (member + j % quad) % quad
-        gather_rows(to_y * quad + to_member, send.at[j])
-        row_copy(j).start()
-        return c
-
-    lax.fori_loop(1, lists, route, 0)
+        prepare(i)
+        row_copy(order(i)).start()
+        return c
+
+    def hold(i, c):
+        prepare(i)
+        return c
+
+    lax.fori_loop(0, AHEAD, route, 0)
+    lax.fori_loop(AHEAD, lists - 1, hold, 0)
     gather_rows(y * quad + member, recv.at[0])
 
     @pl.when(core == home)
@@ -157,11 +178,17 @@
 
     def take(i, c):
         j = order(i)
+        row_copy(j).wait_send()
+
+        @pl.when(i + AHEAD < lists - 1)
+        def _():
+            row_copy(order(i + AHEAD)).start()
+
         row_copy(j).wait_recv()
         add_block(j)
         return c
 
-    lax.fori_loop(1, lists, take, 0)
+    lax.fori_loop(0, lists - 1, take, 0)
 
     eye = iota((share, 128), 0) == iota((share, 128), 1)
 
@@ -243,12 +270,6 @@
     def _():
         cent_far.wait_send()
 
-    def sent_rows(i, c):
-        row_copy(order(i)).wait_send()
-        return c
-
-    lax.fori_loop(1, lists, sent_rows, 0)
-
     def sent_parts(t, c):
         part_copy(t).wait_send()
         return c
@@ -262,8 +283,9 @@
             pltpu.make_async_copy(mfin.at[i], mfin.at[i], mf_recv.at[i]),
         ]
 
+    own_in.wait()
     for h in range(local_lists):
-        sums = cent_ref[h, fine_rows(sh), :].astype(F32) * PRIOR
+        sums = own_s[h].astype(F32) * PRIOR
         mass = jnp.zeros((1, 128), F32)
         for k in range(groups):
             i = h * groups + k
@@ -304,9 +326,11 @@
         return pl.pallas_call(
             functools.partial(kernel, n_list, n_shard, full),
             out_shape=jax.ShapeDtypeStruct((local_lists, share, width), F32),
-            in_specs=[vmem, vmem, vmem],
+            in_specs=[vmem, pl.BlockSpec(memory_space=pl.ANY), pl.BlockSpec(memory_space=pl.ANY)],
             out_specs=vmem,
             scratch_shapes=[
+                pltpu.VMEM((rows, width), BF16),
+                pltpu.VMEM((local_lists, share, width), BF16),
                 pltpu.VMEM((rows // cap, cap), F32),
                 pltpu.VMEM((lists, cap, sent), BF16),
                 pltpu.VMEM((lists, cap, sent), BF16),
@@ -321,6 +345,7 @@
                 pltpu.VMEM((halves, 8, 128), F32),
                 pltpu.VMEM((arrivals, share, width), BF16),
                 pltpu.VMEM((arrivals, 8, 128), F32),
+                dma((2,)),
                 dma((3,)),
                 dma((lists,)),
                 dma((lists,)),
@@ -338,7 +363,7 @@
             cost_estimate=pl.CostEstimate(
                 flops=flops, bytes_accessed=4 * rows * width, transcendentals=lists * cap * fine
             ),
-        )(list_ids.reshape(rows // cap, cap), embeddings, centroids)
+        )(list_ids.T, embeddings, centroids)
 
     placed = (P(("list", "shard"), None), P(("list", "shard"), None), P("list", None, None))
     return jax.shard_map(

time: 78.7 us -> 69.6 us (0.88)
  the two profiles are of different devices: /device:TPU:12 before, /device:TPU:17 now
where the time goes in v2:
time: 69.6 us; the launch traced here: 69.4 us
  Pallas kernels  67.8 us (97%)
  local copies, waits for them, and re-layouts  1.58 us (2%)
    pallas_call x1, Pallas kernels, per_device(): pl.pallas_call(functools.partial(kernel, n_list, n_shard, full), out_shap...  67.8 us
    unnamed x3, local copies, waits for them, and re-layouts  1.58 us

profile of v2, /device:TPU:17, one launch (start us, length us, event | category | flops | bytes accessed | tf_op | source)
XLA Modules:
  0.0 69.4 jit_solution(15229143876260871150)
XLA Ops:
  0.0 0.0 copy-start
  0.0 0.7 %copy-done = s32[2048,1]{0,1:T(1,128)S(1)} copy-done((s32[2048,1]{0,1:T(1,128)S(1)}, s32[2048,1]{0,1:T(1,128)}, u32[]{:S(2)}) %copy-start) | copy-done | bytes 8216
  0.7 67.8 %shard_map.37 = f32[2,128,768]{2,1,0:T(8,128)S(1)} custom-call(s32[1,2048]{1,0:T(1,128)S(1)} %bitcast.1, bf16[2048,768]{1,0:T(8,128)(2,1)} %emb_ref.1, bf16[2,1024,768]{2,1,0:T(8,128)(2,1)} %cent_ref.1), custom_call_target="tpu_custom_call" | custom-call | flops 12884901888 | bytes 6291456 | tf_op jit(solution)/shard_map/pallas_call | solution.py:326
  68.5 0.9 %copy.5 = f32[2,128,768]{2,1,0:T(8,128)} copy(f32[2,128,768]{2,1,0:T(8,128)S(1)} %shard_map.37) | data formatting | bytes 1572864
Async XLA Ops:
  0.0 0.7 %copy-start = (s32[2048,1]{0,1:T(1,128)S(1)}, s32[2048,1]{0,1:T(1,128)}, u32[]{:S(2)}) copy-start(s32[2048,1]{0,1:T(1,128)} %param.4) | copy-start | bytes 24580

commit v3 on v2

--- a/solution.py
+++ b/solution.py
@@ -13,7 +13,7 @@
 F32 = jnp.float32
 BF16 = jnp.bfloat16
 CORES = 2
-AHEAD = 3
+AHEAD = 4
 
 
 def iota(shape, axis):
@@ -27,19 +27,20 @@
 def kernel(
     n_list, n_shard, full,
     ids_ref, emb_ref, cent_ref, out_ref,
-    emb_s, own_s, slot_s, send, recv, cbuf, csq, acc,
+    emb_s, own_s, resp_s, slot_s, send, recv, cbuf, csq, acc,
     part, mpart, other, mother, merged, mmerged, fin, mfin,
     in_sem, cent_sem, p1_send, p1_recv, part_send, part_recv, mp_sem,
     fin_send, fin_recv, mf_send, mf_recv,
 ):
-    local_lists, fine, width = cent_ref.shape
+    local_lists, _, _, share, width = cent_ref.shape
+    fine = n_shard * share
     quad = local_lists * CORES
     planes = n_list // CORES
     lists = planes * quad
     groups = n_shard // quad
     halves = n_shard // CORES
     per_group = quad // CORES
-    share = fine // n_shard
+    half = halves * share
     rows = emb_ref.shape[0]
     cap = rows // 8
     li, sh = lax.axis_index("list"), lax.axis_index("shard")
@@ -49,9 +50,7 @@
     partner = {"list": y * CORES + (1 - core), "shard": sh}
 
     emb_in = pltpu.make_async_copy(emb_ref, emb_s, in_sem.at[0])
-    own_in = pltpu.make_async_copy(
-        cent_ref.at[:, pl.ds(pl.multiple_of(sh * share, share), share), :], own_s, in_sem.at[1]
-    )
+    own_in = pltpu.make_async_copy(cent_ref.at[:, sh // CORES, sh % CORES], own_s, in_sem.at[1])
     emb_in.start()
     own_in.start()
 
@@ -94,16 +93,21 @@
     emb_in.wait()
     pl.semaphore_wait(barrier, in_plane - 1 + (planes - 1) * quad)
 
-    cent_far = pltpu.make_async_remote_copy(
-        src_ref=cent_ref.at[hidx], dst_ref=cbuf, send_sem=cent_sem.at[0], recv_sem=cent_sem.at[1],
-        device_id=partner, device_id_type=MESH,
-    )
-    cent_near = pltpu.make_async_copy(cent_ref.at[hidx], cbuf, cent_sem.at[2])
+    cent_far = [
+        pltpu.make_async_remote_copy(
+            src_ref=cent_ref.at[hidx, :, p], dst_ref=cbuf.at[p], send_sem=cent_sem.at[0, p], recv_sem=cent_sem.at[1, p],
+            device_id=partner, device_id_type=MESH,
+        )
+        for p in range(CORES)
+    ]
+    cent_near = [
+        pltpu.make_async_copy(cent_ref.at[hidx, :, p], cbuf.at[p], cent_sem.at[2, p]) for p in range(CORES)
+    ]
 
     @pl.when(core == home)
     def _():
-        cent_far.start()
-        cent_near.start()
+        for copy in cent_far + cent_near:
+            copy.start()
 
     def gather_rows(l, dst):
         base = (l * cap).astype(F32)
@@ -149,54 +153,71 @@
 
     @pl.when(core == home)
     def _():
-        cent_near.wait()
+        for copy in cent_near:
+            copy.wait()
 
     @pl.when(core != home)
     def _():
-        cent_far.wait_recv()
+        for copy in cent_far:
+            copy.wait_recv()
 
     def square(i, c):
-        at = pl.ds(pl.multiple_of(i * 128, 128), 128)
-        some = cbuf[at, :].astype(F32)
-        csq[at, :] = jnp.broadcast_to((0.5 * SHARP) * jnp.sum(some * some, axis=1, keepdims=True), (128, cap))
-        return c
-
-    lax.fori_loop(0, fine // 128, square, 0)
+        at = pl.ds(pl.multiple_of(i * share, share), share)
+        some = cbuf[i // halves, i % halves].astype(F32)
+        csq[at, :] = jnp.broadcast_to((0.5 * SHARP) * jnp.sum(some * some, axis=1, keepdims=True), (share, cap))
+        return c
+
+    lax.fori_loop(0, n_shard, square, 0)
     acc[...] = jnp.zeros_like(acc)
 
-    def add_block(j):
-        x = recv[j, :, :width]
-        flags = jnp.ones((cap, 128), BF16) if full else recv[j, :, width:]
-        raw = lax.dot_general(cbuf[...], x, (((1,), (1,)), ((), ())), preferred_element_type=F32)
+    def responses(j):
+        cents = cbuf[...].reshape(fine, width)
+        raw = lax.dot_general(
+            cents, recv[j, :, :width], (((1,), (1,)), ((), ())), preferred_element_type=F32
+        )
         scores = SHARP * raw - csq[...]
         grown = jnp.exp(scores - jnp.max(scores, axis=0, keepdims=True))
-        resp = (grown * (1.0 / jnp.sum(grown, axis=0, keepdims=True))).astype(BF16)
-        acc[:, :width] += dot(resp, x)
-        acc[:, width:] += dot(resp, flags)
-
-    add_block(0)
-
-    def take(i, c):
-        j = order(i)
-        row_copy(j).wait_send()
+        return (grown * (1.0 / jnp.sum(grown, axis=0, keepdims=True))).astype(BF16)
+
+    def add(j, at, resp):
+        acc[at, :width] += dot(resp, recv[j, :, :width])
+        acc[at, width:] += dot(resp, jnp.ones((cap, 128), BF16) if full else recv[j, :, width:])
+
+    add(0, slice(None), responses(0))
+
+    def await_rows(i):
+        row_copy(order(i)).wait_send()
 
         @pl.when(i + AHEAD < lists - 1)
         def _():
             row_copy(order(i + AHEAD)).start()
 
-        row_copy(j).wait_recv()
-        add_block(j)
-        return c
-
-    lax.fori_loop(0, lists - 1, take, 0)
+        row_copy(order(i)).wait_recv()
+
+    def take(i, c):
+        await_rows(i)
+        add(order(i), slice(None), responses(order(i)))
+        return c
+
+    lax.fori_loop(0, lists - 2, take, 0)
+
+    final = lists - 2
+    await_rows(final)
+    resp_s[...] = responses(order(final))
+
+    def add_last(p):
+        at = pl.ds(pl.multiple_of(p * half, half), half)
+        add(order(final), at, resp_s[at, :])
+
+    add_last(1 - core)
 
     eye = iota((share, 128), 0) == iota((share, 128), 1)
 
     def pair(t):
         return ((group + 1 + t // per_group) % groups) * per_group + (t + sh // CORES) % per_group
 
-    def fine_rows(shard):
-        return pl.ds(pl.multiple_of(shard * share, share), share)
+    def fine_rows(p, t):
+        return pl.ds(pl.multiple_of(p * half + pair(t) * share, share), share)
 
     def mass_row(at):
         tile = acc[at, width:]
@@ -214,7 +235,7 @@
     )
 
     def give(t, c):
-        at = fine_rows(CORES * pair(t) + (1 - core))
+        at = fine_rows(1 - core, t)
         part[t] = acc[at, :width].astype(BF16)
         part_copy(t).start()
         mpart[t] = mass_row(at)
@@ -222,6 +243,7 @@
 
     lax.fori_loop(0, halves, give, 0)
     mass_copy.start()
+    add_last(core)
 
     def fin_copies(t):
         to = {"list": y * CORES + home, "shard": CORES * pair(t) + core}
@@ -247,7 +269,7 @@
     mass_copy.wait_recv()
 
     def forward(t, c):
-        at = fine_rows(CORES * pair(t) + core)
+        at = fine_rows(core, t)
         part_copy(t).wait_recv()
         merged[t] = (acc[at, :width] + other[t].astype(F32)).astype(BF16)
         mmerged[t] = mass_row(at) + mother[t]
@@ -268,7 +290,8 @@
 
     @pl.when(core == home)
     def _():
-        cent_far.wait_send()
+        for copy in cent_far:
+            copy.wait_send()
 
     def sent_parts(t, c):
         part_copy(t).wait_send()
@@ -331,10 +354,11 @@
             scratch_shapes=[
                 pltpu.VMEM((rows, width), BF16),
                 pltpu.VMEM((local_lists, share, width), BF16),
+                pltpu.VMEM((fine, cap), BF16),
                 pltpu.VMEM((rows // cap, cap), F32),
                 pltpu.VMEM((lists, cap, sent), BF16),
                 pltpu.VMEM((lists, cap, sent), BF16),
-                pltpu.VMEM((fine, width), BF16),
+                pltpu.VMEM((CORES, halves, share, width), BF16),
                 pltpu.VMEM((fine, cap), F32),
                 pltpu.VMEM((fine, width + 128), F32),
                 pltpu.VMEM((halves, share, width), BF16),
@@ -346,7 +370,7 @@
                 pltpu.VMEM((arrivals, share, width), BF16),
                 pltpu.VMEM((arrivals, 8, 128), F32),
                 dma((2,)),
-                dma((3,)),
+                dma((3, CORES)),
                 dma((lists,)),
                 dma((lists,)),
                 dma((halves,)),
@@ -363,7 +387,7 @@
             cost_estimate=pl.CostEstimate(
                 flops=flops, bytes_accessed=4 * rows * width, transcendentals=lists * cap * fine
             ),
-        )(list_ids.T, embeddings, centroids)
+        )(list_ids.T, embeddings, centroids.reshape(local_lists, halves, CORES, share, width))
 
     placed = (P(("list", "shard"), None), P(("list", "shard"), None), P("list", None, None))
     return jax.shard_map(

time: 69.6 us -> 68.7 us (0.987)
  the two profiles are of different devices: /device:TPU:17 before, /device:TPU:12 now
where the time goes in v3:
time: 68.7 us; the launch traced here: 67.5 us
  Pallas kernels  65.9 us (96%)
  local copies, waits for them, and re-layouts  1.58 us (2%)
    pallas_call x1, Pallas kernels, per_device(): pl.pallas_call(functools.partial(kernel, n_list, n_shard, full), out_shap...  65.9 us
    unnamed x3, local copies, waits for them, and re-layouts  1.58 us

profile of v3, /device:TPU:12, one launch (start us, length us, event | category | flops | bytes accessed | tf_op | source)
XLA Modules:
  0.0 67.5 jit_solution(11397891171073797916)
XLA Ops:
  0.0 0.0 copy-start
  0.0 0.7 %copy-done = s32[2048,1]{0,1:T(1,128)S(1)} copy-done((s32[2048,1]{0,1:T(1,128)S(1)}, s32[2048,1]{0,1:T(1,128)}, u32[]{:S(2)}) %copy-start) | copy-done | bytes 8216
  0.7 65.9 %shard_map.37 = f32[2,128,768]{2,1,0:T(8,128)S(1)} custom-call(s32[1,2048]{1,0:T(1,128)S(1)} %bitcast.2, bf16[2048,768]{1,0:T(8,128)(2,1)} %emb_ref.1, bf16[2,4,2,128,768]{4,3,2,1,0:T(8,128)(2,1)} %bitcast.3), custom_call_target="tpu_custom_call" | custom-call | flops 12884901888 | bytes 6291456 | tf_op jit(solution)/shard_map/pallas_call | solution.py:349
  66.6 0.9 %copy.5 = f32[2,128,768]{2,1,0:T(8,128)} copy(f32[2,128,768]{2,1,0:T(8,128)S(1)} %shard_map.37) | data formatting | bytes 1572864
Async XLA Ops:
  0.0 0.7 %copy-start = (s32[2048,1]{0,1:T(1,128)S(1)}, s32[2048,1]{0,1:T(1,128)}, u32[]{:S(2)}) copy-start(s32[2048,1]{0,1:T(1,128)} %param.4) | copy-start | bytes 24580

commit v4 on v3

--- a/solution.py
+++ b/solution.py
@@ -91,7 +91,6 @@
     slot_s[...] = slot
 
     emb_in.wait()
-    pl.semaphore_wait(barrier, in_plane - 1 + (planes - 1) * quad)
 
     cent_far = [
         pltpu.make_async_remote_copy(
@@ -106,18 +105,24 @@
 
     @pl.when(core == home)
     def _():
-        for copy in cent_far + cent_near:
+        for copy in cent_near:
             copy.start()
 
-    def gather_rows(l, dst):
-        base = (l * cap).astype(F32)
-        place = iota((cap, lane), 0).astype(F32) + base
-        pick = jnp.concatenate(
-            [jnp.where(place == slot_s[b:b + 1, :], 1.0, 0.0).astype(BF16) for b in range(blocks)], axis=1
-        )
-        dst[:, :width] = dot(pick, emb_s[...]).astype(BF16)
+    def gather_rows(first, second):
+        place = iota((cap, lane), 0).astype(F32)
+        picks = []
+        for l in (first, second):
+            base = place + (l * cap).astype(F32)
+            picks.append(
+                jnp.concatenate(
+                    [jnp.where(base == slot_s[b:b + 1, :], 1.0, 0.0).astype(BF16) for b in range(blocks)], axis=1
+                )
+            )
+        pick = jnp.concatenate(picks, axis=0)
+        out = dot(pick, emb_s[...]).astype(BF16)
         if not full:
-            dst[:, width:] = dot(pick, jnp.ones((rows, 128), BF16)).astype(BF16)
+            out = jnp.concatenate([out, dot(pick, jnp.ones((rows, 128), BF16)).astype(BF16)], axis=1)
+        return out
 
     def order(i):
         return lists // 2 + i // 2 - (i % 2) * (2 * (i // 2) + 1)
@@ -127,29 +132,50 @@
         to_member = ((member // 2 + flip // 2) % (quad // 2)) * 2 + (member + flip) % 2
         return (y + j // quad) % planes, to_member
 
-    def row_copy(j):
-        to_y, to_member = target(j)
+    def row_copy(i):
+        to_y, to_member = target(order(i))
         return pltpu.make_async_remote_copy(
-            src_ref=send.at[j], dst_ref=recv.at[j], send_sem=p1_send.at[j], recv_sem=p1_recv.at[j],
+            src_ref=send.at[i], dst_ref=recv.at[i], send_sem=p1_send.at[i], recv_sem=p1_recv.at[i],
             device_id={"list": to_y * CORES + core, "shard": group * quad + to_member}, device_id_type=MESH,
         )
 
-    def prepare(i):
+    def list_of(i):
         to_y, to_member = target(order(i))
-        gather_rows(to_y * quad + to_member, send.at[order(i)])
-
-    def route(i, c):
-        prepare(i)
-        row_copy(order(i)).start()
-        return c
-
-    def hold(i, c):
-        prepare(i)
-        return c
-
-    lax.fori_loop(0, AHEAD, route, 0)
-    lax.fori_loop(AHEAD, lists - 1, hold, 0)
-    gather_rows(y * quad + member, recv.at[0])
+        return to_y * quad + to_member
+
+    def prepare(p):
+        found = gather_rows(list_of(2 * p), list_of(2 * p + 1))
+        send[2 * p] = found[:cap]
+        send[2 * p + 1] = found[cap:]
+
+    def start_rows(p):
+        row_copy(2 * p).start()
+        row_copy(2 * p + 1).start()
+
+    pairs = lists // 2
+    prepare(0)
+    pl.semaphore_wait(barrier, in_plane - 1 + (planes - 1) * quad)
+    start_rows(0)
+
+    @pl.when(core == home)
+    def _():
+        for copy in cent_far:
+            copy.start()
+
+    def route(p, c):
+        prepare(p)
+        start_rows(p)
+        return c
+
+    def hold(p, c):
+        prepare(p)
+        return c
+
+    lax.fori_loop(1, AHEAD // 2, route, 0)
+    lax.fori_loop(AHEAD // 2, pairs - 1, hold, 0)
+    found = gather_rows(list_of(lists - 2), list_of(lists - 1))
+    send[lists - 2] = found[:cap]
+    recv[lists - 1] = found[cap:]
 
     @pl.when(core == home)
     def _():
@@ -168,48 +194,56 @@
         return c
 
     lax.fori_loop(0, n_shard, square, 0)
-    acc[...] = jnp.zeros_like(acc)
-
-    def responses(j):
+
+    def block(i, n):
+        return recv[pl.ds(i, n), :, :].reshape(n * cap, recv.shape[2])
+
+    def responses(i, n):
         cents = cbuf[...].reshape(fine, width)
-        raw = lax.dot_general(
-            cents, recv[j, :, :width], (((1,), (1,)), ((), ())), preferred_element_type=F32
-        )
-        scores = SHARP * raw - csq[...]
+        x = block(i, n)[:, :width]
+        raw = lax.dot_general(cents, x, (((1,), (1,)), ((), ())), preferred_element_type=F32)
+        scores = SHARP * raw - jnp.concatenate([csq[...]] * n, axis=1)
         grown = jnp.exp(scores - jnp.max(scores, axis=0, keepdims=True))
         return (grown * (1.0 / jnp.sum(grown, axis=0, keepdims=True))).astype(BF16)
 
-    def add(j, at, resp):
-        acc[at, :width] += dot(resp, recv[j, :, :width])
-        acc[at, width:] += dot(resp, jnp.ones((cap, 128), BF16) if full else recv[j, :, width:])
-
-    add(0, slice(None), responses(0))
-
-    def await_rows(i):
-        row_copy(order(i)).wait_send()
-
-        @pl.when(i + AHEAD < lists - 1)
-        def _():
-            row_copy(order(i + AHEAD)).start()
-
-        row_copy(order(i)).wait_recv()
-
-    def take(i, c):
-        await_rows(i)
-        add(order(i), slice(None), responses(order(i)))
-        return c
-
-    lax.fori_loop(0, lists - 2, take, 0)
+    def terms(i, n, resp):
+        found = block(i, n)
+        flags = jnp.ones((n * cap, 128), BF16) if full else found[:, width:]
+        return dot(resp, found[:, :width]), dot(resp, flags)
+
+    def add(i, n, at, resp):
+        sums, mass = terms(i, n, resp)
+        acc[at, :width] += sums
+        acc[at, width:] += mass
+
+    sums, mass = terms(lists - 1, 1, responses(lists - 1, 1))
+    acc[:, :width] = sums
+    acc[:, width:] = mass
+
+    def take(p, c):
+        for i in (2 * p, 2 * p + 1):
+            row_copy(i).wait_send()
+
+            @pl.when(i + AHEAD < lists - 1)
+            def _():
+                row_copy(i + AHEAD).start()
+
+        row_copy(2 * p).wait_recv()
+        row_copy(2 * p + 1).wait_recv()
+        add(2 * p, 2, slice(None), responses(2 * p, 2))
+        return c
+
+    lax.fori_loop(0, pairs - 1, take, 0)
 
     final = lists - 2
-    await_rows(final)
-    resp_s[...] = responses(order(final))
-
-    def add_last(p):
-        at = pl.ds(pl.multiple_of(p * half, half), half)
-        add(order(final), at, resp_s[at, :])
-
-    add_last(1 - core)
+    row_copy(final).wait_send()
+    row_copy(final).wait_recv()
+    resp_s[...] = responses(final, 1)
+
+    def add_last(p, step):
+        to_group = (group + 1 + step) % groups
+        at = pl.ds(pl.multiple_of(p * half + to_group * per_group * share, share), per_group * share)
+        add(final, 1, at, resp_s[at, :])
 
     eye = iota((share, 128), 0) == iota((share, 128), 1)
 
@@ -229,21 +263,19 @@
             device_id=partner, device_id_type=MESH,
         )
 
-    mass_copy = pltpu.make_async_remote_copy(
-        src_ref=mpart, dst_ref=mother, send_sem=mp_sem.at[0], recv_sem=mp_sem.at[1],
-        device_id=partner, device_id_type=MESH,
-    )
+    def mass_copy(t):
+        return pltpu.make_async_remote_copy(
+            src_ref=mpart.at[t], dst_ref=mother.at[t], send_sem=mp_sem.at[0, t], recv_sem=mp_sem.at[1, t],
+            device_id=partner, device_id_type=MESH,
+        )
 
     def give(t, c):
         at = fine_rows(1 - core, t)
         part[t] = acc[at, :width].astype(BF16)
         part_copy(t).start()
         mpart[t] = mass_row(at)
-        return c
-
-    lax.fori_loop(0, halves, give, 0)
-    mass_copy.start()
-    add_last(core)
+        mass_copy(t).start()
+        return c
 
     def fin_copies(t):
         to = {"list": y * CORES + home, "shard": CORES * pair(t) + core}
@@ -266,11 +298,10 @@
     def is_own(t):
         return (home == core) & (CORES * pair(t) + core == sh)
 
-    mass_copy.wait_recv()
-
     def forward(t, c):
         at = fine_rows(core, t)
         part_copy(t).wait_recv()
+        mass_copy(t).wait_recv()
         merged[t] = (acc[at, :width] + other[t].astype(F32)).astype(BF16)
         mmerged[t] = mass_row(at) + mother[t]
 
@@ -286,7 +317,19 @@
 
         return c
 
-    lax.fori_loop(0, halves, forward, 0)
+    def far_step(step, c):
+        add_last(1 - core, step)
+        lax.fori_loop(step * per_group, (step + 1) * per_group, give, 0)
+        add_last(core, step)
+        return c
+
+    far = (groups - 1) * per_group
+    lax.fori_loop(0, groups - 1, far_step, 0)
+    add_last(1 - core, groups - 1)
+    lax.fori_loop(far, halves, give, 0)
+    lax.fori_loop(0, far, forward, 0)
+    add_last(core, groups - 1)
+    lax.fori_loop(far, halves, forward, 0)
 
     @pl.when(core == home)
     def _():
@@ -295,10 +338,10 @@
 
     def sent_parts(t, c):
         part_copy(t).wait_send()
+        mass_copy(t).wait_send()
         return c
 
     lax.fori_loop(0, halves, sent_parts, 0)
-    mass_copy.wait_send()
 
     def arrived(i):
         return [
@@ -307,17 +350,19 @@
         ]
 
     own_in.wait()
-    for h in range(local_lists):
-        sums = own_s[h].astype(F32) * PRIOR
-        mass = jnp.zeros((1, 128), F32)
-        for k in range(groups):
-            i = h * groups + k
+    mass = [jnp.zeros((1, 128), F32) for _ in range(local_lists)]
+    for k in range(groups):
+        for h in range(local_lists):
+            i = h * groups + (group + k) % groups
             for copy in arrived(i):
                 copy.wait()
-            sums = sums + fin[i].astype(F32)
-            mass = mass + mfin[i, 0:1, :]
-        column = jnp.sum(jnp.where(eye, mass, 0.0), axis=1, keepdims=True)
-        out_ref[h] = sums / (column + PRIOR)
+            so_far = own_s[h].astype(F32) * PRIOR if k == 0 else out_ref[h]
+            so_far = so_far + fin[i].astype(F32)
+            mass[h] = mass[h] + mfin[i, 0:1, :]
+            if k == groups - 1:
+                column = jnp.sum(jnp.where(eye, mass[h], 0.0), axis=1, keepdims=True)
+                so_far = so_far / (column + PRIOR)
+            out_ref[h] = so_far
 
     def sent_fin(t, c):
         @pl.when(jnp.logical_not(is_own(t)))
@@ -375,7 +420,7 @@
                 dma((lists,)),
                 dma((halves,)),
                 dma((halves,)),
-                dma((2,)),
+                dma((2, halves)),
                 dma((halves,)),
                 dma((arrivals,)),
                 dma((halves,)),

time: 68.7 us -> 69.4 us (1.010); the launches traced: 67.5 us -> 69.2 us
  Pallas kernels: 65.9 us -> 67.6 us
    pallas_call x1, Pallas kernels: 65.9 us -> 67.6 us  [per_device(): pl.pallas_call(functools.partial(kernel, n_list, n_shard, full), out_shap...]
where the time goes in v4:
time: 69.4 us; the launch traced here: 69.2 us
  Pallas kernels  67.6 us (97%)
  local copies, waits for them, and re-layouts  1.58 us (2%)
    pallas_call x1, Pallas kernels, per_device(): pl.pallas_call(functools.partial(kernel, n_list, n_shard, full), out_shap...  67.6 us
    unnamed x3, local copies, waits for them, and re-layouts  1.58 us

profile of v4, /device:TPU:12, one launch (start us, length us, event | category | flops | bytes accessed | tf_op | source)
XLA Modules:
  0.0 69.2 jit_solution(1467869096354780448)
XLA Ops:
  0.0 0.0 copy-start
  0.0 0.7 %copy-done = s32[2048,1]{0,1:T(1,128)S(1)} copy-done((s32[2048,1]{0,1:T(1,128)S(1)}, s32[2048,1]{0,1:T(1,128)}, u32[]{:S(2)}) %copy-start) | copy-done | bytes 8216
  0.7 67.6 %shard_map.37 = f32[2,128,768]{2,1,0:T(8,128)S(1)} custom-call(s32[1,2048]{1,0:T(1,128)S(1)} %bitcast.2, bf16[2048,768]{1,0:T(8,128)(2,1)} %emb_ref.1, bf16[2,4,2,128,768]{4,3,2,1,0:T(8,128)(2,1)} %bitcast.3), custom_call_target="tpu_custom_call" | custom-call | flops 12884901888 | bytes 6291456 | tf_op jit(solution)/shard_map/pallas_call | solution.py:394
  68.3 0.9 %copy.5 = f32[2,128,768]{2,1,0:T(8,128)} copy(f32[2,128,768]{2,1,0:T(8,128)S(1)} %shard_map.37) | data formatting | bytes 1572864
Async XLA Ops:
  0.0 0.7 %copy-start = (s32[2048,1]{0,1:T(1,128)S(1)}, s32[2048,1]{0,1:T(1,128)}, u32[]{:S(2)}) copy-start(s32[2048,1]{0,1:T(1,128)} %param.4) | copy-start | bytes 24580

commit v5 on v4

--- a/solution.py
+++ b/solution.py
@@ -108,10 +108,10 @@
         for copy in cent_near:
             copy.start()
 
-    def gather_rows(first, second):
+    def gather_rows(*wanted):
         place = iota((cap, lane), 0).astype(F32)
         picks = []
-        for l in (first, second):
+        for l in wanted:
             base = place + (l * cap).astype(F32)
             picks.append(
                 jnp.concatenate(
@@ -153,9 +153,11 @@
         row_copy(2 * p + 1).start()
 
     pairs = lists // 2
-    prepare(0)
+    send[0] = gather_rows(list_of(0))
     pl.semaphore_wait(barrier, in_plane - 1 + (planes - 1) * quad)
-    start_rows(0)
+    row_copy(0).start()
+    send[1] = gather_rows(list_of(1))
+    row_copy(1).start()
 
     @pl.when(core == home)
     def _():
@@ -233,7 +235,14 @@
         add(2 * p, 2, slice(None), responses(2 * p, 2))
         return c
 
-    lax.fori_loop(0, pairs - 1, take, 0)
+    def take_one(i, c):
+        row_copy(i).wait_send()
+        row_copy(i).wait_recv()
+        add(i, 1, slice(None), responses(i, 1))
+        return c
+
+    lax.fori_loop(0, pairs - 2, take, 0)
+    lax.fori_loop(lists - 4, lists - 2, take_one, 0)
 
     final = lists - 2
     row_copy(final).wait_send()

time: 69.4 us -> 69.6 us (level)
  no operation moved by 1% of the time
where the time goes in v5:
time: 69.6 us; the launch traced here: 69.3 us
  Pallas kernels  67.7 us (97%)
  local copies, waits for them, and re-layouts  1.58 us (2%)
    pallas_call x1, Pallas kernels, per_device(): pl.pallas_call(functools.partial(kernel, n_list, n_shard, full), out_shap...  67.7 us
    unnamed x3, local copies, waits for them, and re-layouts  1.58 us

profile of v5, /device:TPU:12, one launch (start us, length us, event | category | flops | bytes accessed | tf_op | source)
XLA Modules:
  0.0 69.3 jit_solution(10896553853593808074)
XLA Ops:
  0.0 0.0 copy-start
  0.0 0.7 %copy-done = s32[2048,1]{0,1:T(1,128)S(1)} copy-done((s32[2048,1]{0,1:T(1,128)S(1)}, s32[2048,1]{0,1:T(1,128)}, u32[]{:S(2)}) %copy-start) | copy-done | bytes 8216
  0.7 67.7 %shard_map.37 = f32[2,128,768]{2,1,0:T(8,128)S(1)} custom-call(s32[1,2048]{1,0:T(1,128)S(1)} %bitcast.2, bf16[2048,768]{1,0:T(8,128)(2,1)} %emb_ref.1, bf16[2,4,2,128,768]{4,3,2,1,0:T(8,128)(2,1)} %bitcast.3), custom_call_target="tpu_custom_call" | custom-call | flops 12884901888 | bytes 6291456 | tf_op jit(solution)/shard_map/pallas_call | solution.py:403
  68.4 0.9 %copy.5 = f32[2,128,768]{2,1,0:T(8,128)} copy(f32[2,128,768]{2,1,0:T(8,128)S(1)} %shard_map.37) | data formatting | bytes 1572864
Async XLA Ops:
  0.0 0.7 %copy-start = (s32[2048,1]{0,1:T(1,128)S(1)}, s32[2048,1]{0,1:T(1,128)}, u32[]{:S(2)}) copy-start(s32[2048,1]{0,1:T(1,128)} %param.4) | copy-start | bytes 24580

commit v6 on v3

--- a/solution.py
+++ b/solution.py
@@ -13,7 +13,7 @@
 F32 = jnp.float32
 BF16 = jnp.bfloat16
 CORES = 2
-AHEAD = 4
+AHEAD = 7
 
 
 def iota(shape, axis):

time: 68.7 us -> 68.7 us (level)
  no operation moved by 1% of the time
where the time goes in v6:
time: 68.7 us; the launch traced here: 67.5 us
  Pallas kernels  65.9 us (96%)
  local copies, waits for them, and re-layouts  1.58 us (2%)
    pallas_call x1, Pallas kernels, per_device(): pl.pallas_call(functools.partial(kernel, n_list, n_shard, full), out_shap...  65.9 us
    unnamed x3, local copies, waits for them, and re-layouts  1.58 us

profile of v6, /device:TPU:12, one launch (start us, length us, event | category | flops | bytes accessed | tf_op | source)
XLA Modules:
  0.0 67.5 jit_solution(726966344432539048)
XLA Ops:
  0.0 0.0 copy-start
  0.0 0.7 %copy-done = s32[2048,1]{0,1:T(1,128)S(1)} copy-done((s32[2048,1]{0,1:T(1,128)S(1)}, s32[2048,1]{0,1:T(1,128)}, u32[]{:S(2)}) %copy-start) | copy-done | bytes 8216
  0.7 65.9 %shard_map.37 = f32[2,128,768]{2,1,0:T(8,128)S(1)} custom-call(s32[1,2048]{1,0:T(1,128)S(1)} %bitcast.2, bf16[2048,768]{1,0:T(8,128)(2,1)} %emb_ref.1, bf16[2,4,2,128,768]{4,3,2,1,0:T(8,128)(2,1)} %bitcast.3), custom_call_target="tpu_custom_call" | custom-call | flops 12884901888 | bytes 6291456 | tf_op jit(solution)/shard_map/pallas_call | solution.py:349
  66.6 0.9 %copy.5 = f32[2,128,768]{2,1,0:T(8,128)} copy(f32[2,128,768]{2,1,0:T(8,128)S(1)} %shard_map.37) | data formatting | bytes 1572864
Async XLA Ops:
  0.0 0.7 %copy-start = (s32[2048,1]{0,1:T(1,128)S(1)}, s32[2048,1]{0,1:T(1,128)}, u32[]{:S(2)}) copy-start(s32[2048,1]{0,1:T(1,128)} %param.4) | copy-start | bytes 24580

commit v7 on v3

--- a/solution.py
+++ b/solution.py
@@ -91,7 +91,6 @@
     slot_s[...] = slot
 
     emb_in.wait()
-    pl.semaphore_wait(barrier, in_plane - 1 + (planes - 1) * quad)
 
     cent_far = [
         pltpu.make_async_remote_copy(
@@ -104,11 +103,6 @@
         pltpu.make_async_copy(cent_ref.at[hidx, :, p], cbuf.at[p], cent_sem.at[2, p]) for p in range(CORES)
     ]
 
-    @pl.when(core == home)
-    def _():
-        for copy in cent_far + cent_near:
-            copy.start()
-
     def gather_rows(l, dst):
         base = (l * cap).astype(F32)
         place = iota((cap, lane), 0).astype(F32) + base
@@ -147,7 +141,16 @@
         prepare(i)
         return c
 
-    lax.fori_loop(0, AHEAD, route, 0)
+    prepare(0)
+    pl.semaphore_wait(barrier, in_plane - 1 + (planes - 1) * quad)
+    row_copy(order(0)).start()
+
+    @pl.when(core == home)
+    def _():
+        for copy in cent_far + cent_near:
+            copy.start()
+
+    lax.fori_loop(1, AHEAD, route, 0)
     lax.fori_loop(AHEAD, lists - 1, hold, 0)
     gather_rows(y * quad + member, recv.at[0])
 

time: 68.7 us -> 69.2 us (level)
  Pallas kernels: 65.9 us -> 66.6 us
    pallas_call x1, Pallas kernels: 65.9 us -> 66.6 us  [per_device(): pl.pallas_call(functools.partial(kernel, n_list, n_shard, full), out_shap...]
where the time goes in v7:
time: 69.2 us; the launch traced here: 68.2 us
  Pallas kernels  66.6 us (96%)
  local copies, waits for them, and re-layouts  1.58 us (2%)
    pallas_call x1, Pallas kernels, per_device(): pl.pallas_call(functools.partial(kernel, n_list, n_shard, full), out_shap...  66.6 us
    unnamed x3, local copies, waits for them, and re-layouts  1.58 us

profile of v7, /device:TPU:12, one launch (start us, length us, event | category | flops | bytes accessed | tf_op | source)
XLA Modules:
  0.0 68.2 jit_solution(7948732912420260727)
XLA Ops:
  0.0 0.0 copy-start
  0.0 0.7 %copy-done = s32[2048,1]{0,1:T(1,128)S(1)} copy-done((s32[2048,1]{0,1:T(1,128)S(1)}, s32[2048,1]{0,1:T(1,128)}, u32[]{:S(2)}) %copy-start) | copy-done | bytes 8216
  0.7 66.6 %shard_map.37 = f32[2,128,768]{2,1,0:T(8,128)S(1)} custom-call(s32[1,2048]{1,0:T(1,128)S(1)} %bitcast.2, bf16[2048,768]{1,0:T(8,128)(2,1)} %emb_ref.1, bf16[2,4,2,128,768]{4,3,2,1,0:T(8,128)(2,1)} %bitcast.3), custom_call_target="tpu_custom_call" | custom-call | flops 12884901888 | bytes 6291456 | tf_op jit(solution)/shard_map/pallas_call | solution.py:352
  67.3 0.9 %copy.5 = f32[2,128,768]{2,1,0:T(8,128)} copy(f32[2,128,768]{2,1,0:T(8,128)S(1)} %shard_map.37) | data formatting | bytes 1572864
Async XLA Ops:
  0.0 0.7 %copy-start = (s32[2048,1]{0,1:T(1,128)S(1)}, s32[2048,1]{0,1:T(1,128)}, u32[]{:S(2)}) copy-start(s32[2048,1]{0,1:T(1,128)} %param.4) | copy-start | bytes 24580
